TPU v7x, 256 devices: a whole 4x4x8 slice. The times are simulated.
256 devices in a mesh: wide: 32 (over x, y, core), narrow: 8 (over z).
Axes of the slice: x: 4, y: 4, z: 8, core: 2. Of those that a mesh axis runs over, the one named last changes fastest.
Arguments:
- activity: bfloat16 [256, 8, 512, 512], P(('wide', 'narrow')), may hold values from 0 to 1
- tile_coords: int32 [256, 2], replicated, may hold values from 0 to 31, as said below
- user_owner: int32 [32], replicated, may hold values from 0 to 31, each once
- item_owner: int32 [32], replicated, may hold values from 0 to 31, each once
- user_factor: float32 [16384, 256], P('wide', 'narrow'), may hold values from 0 to 1
- item_factor: float32 [16384, 256], P('wide', 'narrow'), may hold values from 0 to 1
- time_factor: float32 [8, 256], replicated, may hold values from 0.0003 to 0.003
- user_dual: float32 [16384, 256], P('wide', 'narrow'), may hold values from -1.8 to 1.8
- item_dual: float32 [16384, 256], P('wide', 'narrow'), may hold values from -1.8 to 1.8
Outputs:
- new_users: float32 [16384, 256], P('wide', 'narrow')
- new_items: float32 [16384, 256], P('wide', 'narrow')
- new_user_dual: float32 [16384, 256], P('wide', 'narrow')
- new_item_dual: float32 [16384, 256], P('wide', 'narrow')
Inputs may be any that keep to these rules, and one draw needn't show every extreme that they name: `tile_coords`: no pair of blocks appears twice. `user_owner`: each stored row block holds exactly one user block. `item_owner`: each stored row block holds exactly one item block.
All inputs are finite; a program needn't handle non-finite values.
Results may differ from a plain program's by a relative error of at most 0.0017.
The roundings to bfloat16 on the way count: a program that leaves them out, or rounds other values in their place, can miss the bound.
Values may be sent and summed in bfloat16 or wider, within the bound.
A program may use at most 64 MiB of HBM per device.

v0:
```python
import jax
import jax.numpy as jnp
from jax import lax
from jax.experimental import pallas as pl
from jax.experimental.pallas import tpu as pltpu
from jax.sharding import Mesh
from jax.sharding import PartitionSpec as P

RANK = 256
BLOCK = 512
TIMES = 8
PASSES = 2
SIDE = 4
CORES = 2
DEPTH = 8
STEPS = 7
MESH = pl.DeviceIdType.MESH
WIDE = ("wide_0", "wide_1", "wide_2")
WIDE_NARROW = ("wide_0", "wide_1", "wide_2", "narrow")
SEMS = 440
F32 = jnp.float32
BF16 = jnp.bfloat16


def exact_dot(a, b):
    return jnp.dot(a, b, precision=lax.Precision.HIGHEST, preferred_element_type=F32)


def sweep_kernel(
    act_hbm,
    coords,
    user_owner,
    item_owner,
    user_factor,
    item_factor,
    time_factor,
    user_dual,
    item_dual,
    out_users,
    out_items,
    out_user_dual,
    out_item_dual,
    act,
    packed,
    landed,
    held,
    khatri,
    gath,
    zsend,
    kbuf,
    gpart,
    fix,
    fix_land,
    gland,
    gfull,
    base,
    approx,
    partial,
    tland,
    cland,
    dense,
    first_land,
    middle,
    last_land,
    opack,
    oland,
    sems,
    act_sem,
):
    x, y, c, z = (lax.axis_index(name) for name in WIDE_NARROW)
    wide = (x * SIDE + y) * CORES + c
    twin = (x * SIDE + y) * CORES + (1 - c)
    twin_dev = (x, y, 1 - c, z)

    def x_dev(d):
        return (lax.rem(x + d, SIDE), y, c, z)

    def y_dev(d):
        return (x, lax.rem(y + d, SIDE), c, z)

    def z_at(d):
        return lax.rem(z + d, DEPTH)

    def z_dev(d):
        return (x, y, c, z_at(d))

    around = (4, 3, 5, 2, 6, 1, 7)

    load_act = pltpu.make_async_copy(act_hbm.at[0], act, act_sem)
    load_act.start()

    barrier = pltpu.get_barrier_semaphore()
    peers = [x_dev(d) for d in (1, 2, 3)] + [y_dev(d) for d in (1, 2, 3)]
    peers += [z_dev(d) for d in range(1, DEPTH)] + [twin_dev]
    for peer in peers:
        pl.semaphore_signal(barrier, inc=1, device_id=peer, device_id_type=MESH)

    count = [0]
    sent = []

    def send(src, dst, device):
        k = count[0]
        count[0] += 2
        assert count[0] <= SEMS
        copy = pltpu.make_async_remote_copy(
            src_ref=src,
            dst_ref=dst,
            send_sem=sems.at[k],
            recv_sem=sems.at[k + 1],
            device_id=device,
            device_id_type=MESH,
        )
        copy.start()
        sent.append(copy)
        return copy

    def pack(which, ref):
        stacked = jnp.concatenate([ref[:, t * 128 : (t + 1) * 128] for t in range(4)], axis=0)
        packed[which] = stacked.T

    def lines(place, size):
        return pl.ds(pl.multiple_of(place * size, size), size)

    def unpack(which):
        for t in range(4):
            held[which, t * 16 : (t + 1) * 16] = jnp.concatenate(
                [landed[which, n, :, t * 32 : (t + 1) * 32] for n in range(DEPTH)], axis=1
            )

    pack(0, item_factor)
    pl.semaphore_wait(barrier, len(peers))
    lead = [
        send(packed.at[0, lines(z_at(d), 16)], landed.at[0, z], z_dev(d)) for d in around
    ]
    landed[0, z] = packed[0, lines(z, 16)]
    pack(1, item_dual)
    pack(2, user_factor)
    pack(3, user_dual)
    rest = [
        send(packed.at[pl.ds(1, 3), lines(z_at(d), 16)], landed.at[pl.ds(1, 3), z], z_dev(d))
        for d in around
    ]
    for a in (1, 2, 3):
        landed[a, z] = packed[a, lines(z, 16)]
    times = time_factor[...]
    time_gram = exact_dot(times.T, times)
    eye = (
        lax.broadcasted_iota(jnp.int32, (RANK, RANK), 0)
        == lax.broadcasted_iota(jnp.int32, (RANK, RANK), 1)
    ).astype(F32)
    for copy in lead:
        copy.wait_recv()
    unpack(0)

    def unpack_rest():
        for copy in rest:
            copy.wait_recv()
        for a in (1, 2, 3):
            unpack(a)

    def gather(p, rows, after_start, after_middle):
        buf = gath.at[p]
        for h in range(2):
            buf[h, x, y, c] = rows[h * 32 : (h + 1) * 32].astype(BF16)
        starts = [
            send(buf.at[h, x, y, c], buf.at[h, x, y, c], (x_dev, y_dev)[h](d))
            for d in (2, 1, 3)
            for h in range(2)
        ]
        high = rows.astype(BF16)
        low = rows - high.astype(F32)
        missed = lax.dot_general(
            (high.astype(F32) + 0.5 * low).astype(BF16),
            low.astype(BF16),
            (((0,), (0,)), ((), ())),
            preferred_element_type=F32,
        )
        fix[p, 0:RANK] = (missed + missed.T).astype(BF16)
        fixes = [
            send(fix.at[p, lines(lax.rem(x + d, SIDE), 64)], fix_land.at[p, d - 1, 0:64], x_dev(d))
            for d in (2, 1, 3)
        ]
        after_start()
        for copy in starts:
            copy.wait_recv()
        mine = (buf.at[0, :, y, c], buf.at[1, x, :, c])
        middles = [
            (h, d, send(mine[h], mine[h], (y_dev, x_dev)[h](d)))
            for d in (2, 1, 3)
            for h in range(2)
        ]
        twins = [send(mine[h], mine[h], twin_dev) for h in range(2)]
        for copy in fixes:
            copy.wait_recv()
        total = fix[p, lines(x, 64)].astype(F32)
        for d in (1, 2, 3):
            total += fix_land[p, d - 1, 0:64].astype(F32)
        fix[p, RANK : RANK + 64] = total.astype(BF16)
        fixes = [
            send(
                fix.at[p, lines(lax.rem(y + d, SIDE) + 16, 16)],
                fix_land.at[p, d - 1, 64:80],
                y_dev(d),
            )
            for d in (2, 1, 3)
        ]
        after_middle()
        for h, d, copy in sorted(middles, key=lambda entry: (entry[1] + 1) % 4):
            copy.wait_recv()
            if h == 0:
                part = buf.at[0, :, lax.rem(y + SIDE - d, SIDE), c]
            else:
                part = buf.at[1, lax.rem(x + SIDE - d, SIDE), :, c]
            twins.append(send(part, part, twin_dev))
        for copy in fixes:
            copy.wait_recv()
        total = fix[p, lines(y + 16, 16)].astype(F32)
        for d in (1, 2, 3):
            total += fix_land[p, d - 1, 64:80].astype(F32)
        fix[p, RANK + 64 : RANK + 80] = total.astype(BF16)
        twins.append(
            send(fix.at[p, RANK + 64 : RANK + 80], fix_land.at[p, 0, 80:96], twin_dev)
        )
        for copy in twins:
            copy.wait_recv()

    def fetch(p, coord, owner):
        def choose(j):
            place = owner[coords[coord, wide * DEPTH + j]]
            spot = (place // 8, (place // 2) % SIDE, place % CORES)
            for h in range(2):
                zsend[p, j, 2 * h : 2 * h + 2] = gath[p, h, spot[0], spot[1], spot[2]].reshape(
                    2, 16, RANK
                )

        copies = []
        for d in around:
            choose(z_at(d))
            copies.append(send(zsend.at[p, z_at(d)], kbuf.at[p, :, z], z_dev(d)))
        choose(z)
        kbuf[p, :, z] = zsend[p, z]
        return copies

    def gram_start(p):
        total = jnp.zeros((RANK, RANK), F32)
        for h in range(2):
            for a in range(SIDE):
                some = gath[p, h, a].reshape(SIDE * CORES * 32, RANK)
                total += lax.dot_general(
                    some, some, (((0,), (0,)), ((), ())), preferred_element_type=F32
                )
        gpart[p] = total
        own = lines(wide, 8)
        both = fix[p, RANK + 64 : RANK + 80].astype(F32) + fix_land[p, 0, 80:96].astype(F32)
        gpart[p, own] += jnp.where(c == 0, both[0:8], both[8:16])
        copies = [send(gpart.at[p, own], gland.at[p, z], z_dev(d)) for d in around]
        gland[p, z] = gpart[p, own]
        for copy in copies:
            copy.wait_recv()
        gfull[p, x, y, c] = jnp.sum(gland[p], axis=0)
        spot = gfull.at[p, x, y, c]
        copies = [send(spot, spot, x_dev(d)) for d in (2, 1, 3)]
        for copy in copies:
            copy.wait_recv()
        line = gfull.at[p, :, y, c]
        return [send(line, line, y_dev(d)) for d in (2, 1, 3)]

    def gram_end(p, copies):
        for copy in copies:
            copy.wait_recv()
        plane = gfull.at[p, :, :, c]
        send(plane, plane, twin_dev).wait_recv()
        gram = gfull[p].reshape(RANK, RANK) * time_gram
        penalty = jnp.sum(gram * eye) / RANK
        base[...] = gram / penalty + eye
        t = 129.0 / 128.0
        t2 = 2.0 * t * t - 1.0
        approx[...] = (eye * 2.0 - base[...] * (1.0 / 129.0)) * ((t2 + 1.0) / t2 / 129.0)

        def step(_, t):
            t2 = 2.0 * t * t - 1.0
            now = approx[...]
            rest = eye - exact_dot(base[...], now)
            approx[...] = (now + exact_dot(now, rest)) * ((t2 + 1.0) / t2)
            return t2

        lax.fori_loop(0, STEPS, step, F32(t2))
        return penalty

    def tile_half(p, h, forward, khatri_t):
        total = jnp.zeros((BLOCK // 2, RANK), F32)
        cut = slice(h * 256, (h + 1) * 256)
        for k in range(TIMES):
            if forward:
                total += jnp.dot(act[k, cut, :], khatri[k], preferred_element_type=F32)
            else:
                total += jnp.dot(khatri_t[k], act[k, :, cut], preferred_element_type=F32)
        if not forward:
            total = total.T
        partial[p, 2 * h : 2 * h + 2] = total.reshape(2, DEPTH, 16, RANK)
        pair = pl.ds(2 * h, 2)
        copies = [
            (d, send(partial.at[p, pair, z_at(d)], tland.at[p, h, z], z_dev(d))) for d in around
        ]
        tland[p, h, z] = partial[p, 2 * h : 2 * h + 2, z]
        return copies

    def reduced(p, coord, owner, copies):
        twins = [[], []]
        for h in range(2):
            spot = tland.at[p, h, z]
            twins[h].append(send(spot, cland.at[p, h, z], twin_dev))
            for d, copy in copies[h]:
                copy.wait_recv()
                origin = lax.rem(z + DEPTH - d, DEPTH)
                twins[h].append(send(tland.at[p, h, origin], cland.at[p, h, origin], twin_dev))
        targets = [owner[coords[coord, wide * DEPTH + j]] for j in range(DEPTH)]
        twin_targets = [owner[coords[coord, twin * DEPTH + j]] for j in range(DEPTH)]
        firsts = []
        for h in range(2):
            for copy in twins[h]:
                copy.wait_recv()

            def place(i, carry):
                a, b = i // SIDE, i % SIDE
                block = ((a * SIDE + b) if h == 0 else (b * SIDE + a)) * CORES + c
                total = jnp.zeros((2, 16, RANK), F32)
                for j in range(DEPTH):
                    total += tland[p, h, j] * (targets[j] == block).astype(F32)
                    total += cland[p, h, j] * (twin_targets[j] == block).astype(F32)
                dense[p, h, a, b] = total
                return carry

            lax.fori_loop(0, SIDE * SIDE, place, 0)
            me = (x, y)[h]
            for d in (2, 1, 3):
                firsts.append(
                    send(
                        dense.at[p, h, lax.rem(me + d, SIDE)],
                        first_land.at[p, h, d - 1],
                        (x_dev, y_dev)[h](d),
                    )
                )
        seconds = []
        for h in range(2):
            for copy in firsts[3 * h : 3 * h + 3]:
                copy.wait_recv()
            middle[p, h] = (dense[p, h, (x, y)[h]] + first_land[p, h, 0]) + (
                first_land[p, h, 1] + first_land[p, h, 2]
            )
            other = (y, x)[h]
            for d in (2, 1, 3):
                seconds.append(
                    send(
                        middle.at[p, h, lax.rem(other + d, SIDE)],
                        last_land.at[p, h, d - 1],
                        (y_dev, x_dev)[h](d),
                    )
                )
        halves = []
        for h in range(2):
            for copy in seconds[3 * h : 3 * h + 3]:
                copy.wait_recv()
            total = (middle[p, h, (y, x)[h]] + last_land[p, h, 0]) + (
                last_land[p, h, 1] + last_land[p, h, 2]
            )
            halves.append(total.reshape(32, RANK))
        return jnp.concatenate(halves, axis=0)

    def admm(sums, factor, dual, penalty):
        inverse = approx[...]
        for _ in range(PASSES):
            target = exact_dot(sums + penalty * (factor + dual), inverse) / penalty
            factor = jnp.maximum(target - dual, 0.0)
            dual = dual + factor - target
        return factor, dual

    def give_back(p, factor, dual):
        for a, rows in ((0, factor), (1, dual)):
            for n in range(DEPTH):
                opack[p, n, a] = jnp.concatenate(
                    [
                        rows[t * 16 : (t + 1) * 16, n * 32 : (n + 1) * 32]
                        for t in range(4)
                    ],
                    axis=1,
                )
        copies = [send(opack.at[p, z_at(d)], oland.at[p, :, z], z_dev(d)) for d in around]
        oland[p, :, z] = opack[p, z]
        return copies

    def take_back(p, copies, outs):
        for copy in copies:
            copy.wait_recv()
        for a in range(2):
            turned = oland[p, a].reshape(128, 128).T
            for t in range(4):
                outs[a][:, t * 128 : (t + 1) * 128] = turned[t * 32 : (t + 1) * 32, :]

    def update(p, rows, factor_at, dual_at, own_coord, own, other, after_start, after_middle, after_gram):
        forward = p == 0
        gather(p, rows, after_start, after_middle)
        fetched = fetch(p, 1 - own_coord, other)
        gram_copies = gram_start(p)
        after_gram()
        for copy in fetched:
            copy.wait_recv()
        if forward:
            load_act.wait()
        low = kbuf[p].reshape(BLOCK, RANK).astype(F32)
        khatri_t = None
        if forward:
            for k in range(TIMES):
                khatri[k] = (low * times[k : k + 1, :]).astype(BF16)
        else:
            turned = low.T
            columns = times.T
            khatri_t = [(turned * columns[:, k : k + 1]).astype(BF16) for k in range(TIMES)]
        copies = [tile_half(p, h, forward, khatri_t) for h in range(2)]
        penalty = gram_end(p, gram_copies)
        sums = reduced(p, own_coord, own, copies)
        return admm(sums, held[factor_at], held[dual_at], penalty)

    nothing = lambda: None
    users, user_duals = update(
        0, held[0], 2, 3, 0, user_owner, item_owner, nothing, unpack_rest, nothing
    )
    returned = []
    items, item_duals = update(
        1,
        users,
        0,
        1,
        1,
        item_owner,
        user_owner,
        lambda: returned.extend(give_back(0, users, user_duals)),
        nothing,
        lambda: take_back(0, returned, (out_users, out_user_dual)),
    )
    take_back(1, give_back(1, items, item_duals), (out_items, out_item_dual))
    for copy in sent:
        copy.wait_send()


def local(
    activity,
    tile_coords,
    user_owner,
    item_owner,
    user_factor,
    item_factor,
    time_factor,
    user_dual,
    item_dual,
):
    vmem = pl.BlockSpec(memory_space=pltpu.VMEM)
    smem = pl.BlockSpec(memory_space=pltpu.SMEM)
    slab = jax.ShapeDtypeStruct((RANK // DEPTH, BLOCK), F32)
    outs = pl.pallas_call(
        sweep_kernel,
        out_shape=(slab,) * 4,
        in_specs=[pl.BlockSpec(memory_space=pl.ANY), smem, smem, smem] + [vmem] * 5,
        out_specs=(vmem,) * 4,
        scratch_shapes=[
            pltpu.VMEM((TIMES, BLOCK, BLOCK), BF16),
            pltpu.VMEM((4, 128, 128), F32),
            pltpu.VMEM((4, DEPTH, 16, 128), F32),
            pltpu.VMEM((4, 64, RANK), F32),
            pltpu.VMEM((TIMES, BLOCK, RANK), BF16),
            pltpu.VMEM((2, 2, SIDE, SIDE, CORES, 32, RANK), BF16),
            pltpu.VMEM((2, DEPTH, 4, 16, RANK), BF16),
            pltpu.VMEM((2, 4, DEPTH, 16, RANK), BF16),
            pltpu.VMEM((2, RANK, RANK), F32),
            pltpu.VMEM((2, RANK + 80, RANK), BF16),
            pltpu.VMEM((2, SIDE - 1, 96, RANK), BF16),
            pltpu.VMEM((2, DEPTH, 8, RANK), F32),
            pltpu.VMEM((2, SIDE, SIDE, CORES, 8, RANK), F32),
            pltpu.VMEM((RANK, RANK), F32),
            pltpu.VMEM((RANK, RANK), F32),
            pltpu.VMEM((2, 4, DEPTH, 16, RANK), F32),
            pltpu.VMEM((2, 2, DEPTH, 2, 16, RANK), F32),
            pltpu.VMEM((2, 2, DEPTH, 2, 16, RANK), F32),
            pltpu.VMEM((2, 2, SIDE, SIDE, 2, 16, RANK), F32),
            pltpu.VMEM((2, 2, SIDE - 1, SIDE, 2, 16, RANK), F32),
            pltpu.VMEM((2, 2, SIDE, 2, 16, RANK), F32),
            pltpu.VMEM((2, 2, SIDE - 1, 2, 16, RANK), F32),
            pltpu.VMEM((2, DEPTH, 2, 16, 128), F32),
            pltpu.VMEM((2, 2, DEPTH, 16, 128), F32),
            pltpu.SemaphoreType.DMA((SEMS,)),
            pltpu.SemaphoreType.DMA,
        ],
        compiler_params=pltpu.CompilerParams(
            collective_id=0, has_side_effects=True, vmem_limit_bytes=48 * 2**20
        ),
        name="sweep",
    )(
        activity,
        tile_coords.T,
        user_owner,
        item_owner,
        user_factor.T,
        item_factor.T,
        time_factor,
        user_dual.T,
        item_dual.T,
    )
    users, items, user_duals, item_duals = (out.T for out in outs)
    return (users, items, user_duals, item_duals)


def solution(mesh):
    split = Mesh(
        mesh.devices.reshape(SIDE, SIDE, CORES, mesh.shape["narrow"]),
        WIDE_NARROW,
    )
    in_specs = (
        P(WIDE_NARROW, None, None, None),
        P(),
        P(),
        P(),
        P(WIDE, "narrow"),
        P(WIDE, "narrow"),
        P(),
        P(WIDE, "narrow"),
        P(WIDE, "narrow"),
    )
    out_specs = (P(WIDE, "narrow"), P(WIDE, "narrow"), P(WIDE, "narrow"), P(WIDE, "narrow"))
    return jax.shard_map(local, mesh=split, in_specs=in_specs, out_specs=out_specs, check_vma=False)
```

profile of v0, /device:TPU:1, one launch (start us, length us, event | category | flops | bytes accessed | tf_op | source)
XLA Modules:
  0.0 141.6 jit_solution(9088055504382644576)
XLA Ops:
  0.6 0.0 copy-start
  0.6 2.2 %copy-done = bf16[1,8,512,512]{3,2,1,0:T(8,128)(2,1)S(1)} copy-done((bf16[1,8,512,512]{3,2,1,0:T(8,128)(2,1)S(1)}, bf16[1,8,512,512]{3,2,1,0:T(8,128)(2,1)}, u32[]{:S(2)}) %copy-start) | copy-done | bytes 4194328
  2.8 0.0 copy-start.1
  2.8 0.8 copy-done.1
  3.7 0.0 copy-start.2
  3.7 0.8 copy-done.2
  4.5 0.0 copy-start.3
  4.5 0.8 copy-done.3
  5.3 0.0 copy-start.4
  5.3 0.8 copy-done.4
  6.2 0.0 copy-start.5
  6.2 0.7 copy-done.5
  6.9 0.0 copy-start.6
  6.9 0.7 copy-done.6
  7.6 0.0 copy-start.7
  7.6 0.7 copy-done.7
  8.2 0.0 copy-start.8
  8.2 0.7 copy-done.8
  8.9 130.2 %sweep.1 = (f32[32,512]{1,0:T(8,128)S(1)}, f32[32,512]{1,0:T(8,128)S(1)}, f32[32,512]{1,0:T(8,128)S(1)}, f32[32,512]{1,0:T(8,128)S(1)}) custom-call(bf16[1,8,512,512]{3,2,1,0:T(8,128)(2,1)S(1)} %copy-done, s32[2,256]{1,0:T(2,128)S(1)} %bitcast.17, s32[32]{0:T(128)S(1)} %copy-done.7, s32[32]{0:T(128)S(1)} %copy-done.8, f32[32,512]{1,0:T(8,128)S(1)} %bitcast.9, ...), custom_call_target="tpu_custom_call" | custom-call | tf_op jit(solution)/shard_map/sweep/pallas_call | solution.py:460
  139.1 0.6 copy.17
  139.7 0.6 copy.18
  140.3 0.6 copy.19
  141.0 0.6 copy.20
Async XLA Ops:
  0.6 2.2 %copy-start = (bf16[1,8,512,512]{3,2,1,0:T(8,128)(2,1)S(1)}, bf16[1,8,512,512]{3,2,1,0:T(8,128)(2,1)}, u32[]{:S(2)}) copy-start(bf16[1,8,512,512]{3,2,1,0:T(8,128)(2,1)} %act_hbm.1) | copy-start | bytes 12582916
  2.8 0.8 copy-start.1
  3.7 0.8 copy-start.2
  4.5 0.8 copy-start.3
  5.3 0.8 copy-start.4
  6.2 0.7 copy-start.5
  6.9 0.7 copy-start.6
  7.6 0.7 copy-start.7
  8.2 0.7 copy-start.8
where the time goes:
time: 142 us
  Pallas kernels  130 us (92%)
  local copies, waits for them, and re-layouts  10.7 us (8%)
    pallas_call x1, Pallas kernels, local(): pl.pallas_call(sweep_kernel, out_shape=(slab,) * 4, in_specs=[pl.BlockSpe...  130 us
    unnamed x22, local copies, waits for them, and re-layouts  10.7 us

commit v1 on v0

v1 whole, which is shorter than its diff:
```python
import jax
import jax.numpy as jnp
from jax import lax
from jax.experimental import pallas as pl
from jax.experimental.pallas import tpu as pltpu
from jax.sharding import Mesh
from jax.sharding import PartitionSpec as P

RANK = 256
BLOCK = 512
TIMES = 8
PASSES = 2
SIDE = 4
CORES = 2
DEPTH = 8
STEPS = 7
SCALES = [129.0 / 128.0]
for _ in range(STEPS):
    SCALES.append(2.0 * SCALES[-1] ** 2 - 1.0)
MESH = pl.DeviceIdType.MESH
WIDE = ("wide_0", "wide_1", "wide_2")
WIDE_NARROW = ("wide_0", "wide_1", "wide_2", "narrow")
SEMS = 104
F32 = jnp.float32
BF16 = jnp.bfloat16


def exact_dot(a, b):
    return jnp.dot(a, b, precision=lax.Precision.HIGHEST, preferred_element_type=F32)


def sweep_kernel(
    act_hbm,
    coords_hbm,
    user_owner_hbm,
    item_owner_hbm,
    user_factor_hbm,
    item_factor_hbm,
    time_factor_hbm,
    user_dual_hbm,
    item_dual_hbm,
    out_users,
    out_items,
    out_user_duals,
    out_item_duals,
    act,
    coords,
    user_owner,
    item_owner,
    slabs,
    time_factor,
    packed,
    landed,
    held,
    khatri,
    gath,
    zsend,
    kbuf,
    gpart,
    fix,
    fix_land,
    gland,
    gfull,
    base,
    approx,
    partial,
    tland,
    cland,
    dense,
    first_land,
    middle,
    last_land,
    opack,
    oland,
    sems,
    load_sems,
):
    x, y, c, z = (lax.axis_index(name) for name in WIDE_NARROW)
    wide = (x * SIDE + y) * CORES + c
    twin = (x * SIDE + y) * CORES + (1 - c)
    twin_dev = (x, y, 1 - c, z)

    def x_dev(d):
        return (lax.rem(x + d, SIDE), y, c, z)

    def y_dev(d):
        return (x, lax.rem(y + d, SIDE), c, z)

    def z_at(d):
        return lax.rem(z + d, DEPTH)

    def z_dev(d):
        return (x, y, c, z_at(d))

    around = (4, 3, 5, 2, 6, 1, 7)

    barrier = pltpu.get_barrier_semaphore()
    peers = [x_dev(d) for d in (1, 2, 3)] + [y_dev(d) for d in (1, 2, 3)]
    peers += [z_dev(d) for d in range(1, DEPTH)] + [twin_dev]
    for peer in peers:
        pl.semaphore_signal(barrier, inc=1, device_id=peer, device_id_type=MESH)

    moves = (
        (item_factor_hbm, slabs.at[0]),
        (item_dual_hbm, slabs.at[1]),
        (user_factor_hbm, slabs.at[2]),
        (user_dual_hbm, slabs.at[3]),
        (time_factor_hbm, time_factor),
        (coords_hbm, coords),
        (user_owner_hbm, user_owner),
        (item_owner_hbm, item_owner),
        (act_hbm.at[0], act),
    )
    loads = [
        pltpu.make_async_copy(src, dst, load_sems.at[i]) for i, (src, dst) in enumerate(moves)
    ]
    for load in loads:
        load.start()

    groups = []

    class Group:
        def __init__(self, ref):
            k = 2 * len(groups)
            assert k + 1 < SEMS
            groups.append(self)
            self.whole = pltpu.make_async_remote_copy(
                src_ref=ref,
                dst_ref=ref,
                send_sem=sems.at[k],
                recv_sem=sems.at[k + 1],
                device_id=twin_dev,
                device_id_type=MESH,
            )
            self.pair = dict(send_sem=sems.at[k], recv_sem=sems.at[k + 1], device_id_type=MESH)

        def send(self, src, dst, device):
            pltpu.make_async_remote_copy(
                src_ref=src, dst_ref=dst, device_id=device, **self.pair
            ).start()

        def take(self):
            self.whole.wait_recv()

    def pack(which):
        stacked = jnp.concatenate(
            [slabs[which, :, t * 128 : (t + 1) * 128] for t in range(4)], axis=0
        )
        packed[which] = stacked.T

    def lines(place, size):
        return pl.ds(pl.multiple_of(place * size, size), size)

    def unpack(which):
        for t in range(4):
            held[which, t * 16 : (t + 1) * 16] = jnp.concatenate(
                [landed[which, n, :, t * 32 : (t + 1) * 32] for n in range(DEPTH)], axis=1
            )

    loads[0].wait()
    pack(0)
    pl.semaphore_wait(barrier, len(peers))
    lead = Group(landed.at[0, 0:7])
    for d in around:
        lead.send(packed.at[0, lines(z_at(d), 16)], landed.at[0, z], z_dev(d))
    landed[0, z] = packed[0, lines(z, 16)]
    for load in loads[1:8]:
        load.wait()
    for a in (1, 2, 3):
        pack(a)
        landed[a, z] = packed[a, lines(z, 16)]
    times = time_factor[...]
    time_gram = exact_dot(times.T, times)
    eye = (
        lax.broadcasted_iota(jnp.int32, (RANK, RANK), 0)
        == lax.broadcasted_iota(jnp.int32, (RANK, RANK), 1)
    ).astype(F32)
    lead.take()
    unpack(0)

    rest = Group(landed.at[1:4, 0:7])

    def send_rest():
        for d in around:
            rest.send(
                packed.at[1:4, lines(z_at(d), 16)], landed.at[1:4, z], z_dev(d)
            )

    def unpack_rest():
        rest.take()
        for a in (1, 2, 3):
            unpack(a)

    def gather(p, rows, after_start, after_middle):
        buf = gath.at[p]
        for h in range(2):
            buf[h, x, y, c] = rows[h * 32 : (h + 1) * 32].astype(BF16)
        starts = Group(buf.at[0, 0, 0:3])
        for d in (2, 1, 3):
            for h in range(2):
                starts.send(buf.at[h, x, y, c], buf.at[h, x, y, c], (x_dev, y_dev)[h](d))
        high = rows.astype(BF16)
        low = rows - high.astype(F32)
        missed = lax.dot_general(
            (high.astype(F32) + 0.5 * low).astype(BF16),
            low.astype(BF16),
            (((0,), (0,)), ((), ())),
            preferred_element_type=F32,
        )
        fix[p, 0:RANK] = (missed + missed.T).astype(BF16)
        fixes = Group(fix_land.at[p, :, 0:64])
        for d in (2, 1, 3):
            fixes.send(
                fix.at[p, lines(lax.rem(x + d, SIDE), 64)], fix_land.at[p, d - 1, 0:64], x_dev(d)
            )
        after_start()
        starts.take()
        middles = Group(buf.at[0, 0:3])
        mine = (buf.at[0, :, y, c], buf.at[1, x, :, c])
        for d in (2, 1, 3):
            for h in range(2):
                middles.send(mine[h], mine[h], (y_dev, x_dev)[h](d))
        fixes.take()
        total = fix[p, lines(x, 64)].astype(F32)
        for d in (1, 2, 3):
            total += fix_land[p, d - 1, 0:64].astype(F32)
        fix[p, RANK : RANK + 64] = total.astype(BF16)
        fixes = Group(fix_land.at[p, :, 64:80])
        for d in (2, 1, 3):
            fixes.send(
                fix.at[p, lines(lax.rem(y + d, SIDE) + 16, 16)],
                fix_land.at[p, d - 1, 64:80],
                y_dev(d),
            )
        after_middle()
        middles.take()
        twins = Group(buf.at[:, :, :, 0])
        for h in range(2):
            twins.send(buf.at[h, :, :, c], buf.at[h, :, :, c], twin_dev)
        fixes.take()
        total = fix[p, lines(y + 16, 16)].astype(F32)
        for d in (1, 2, 3):
            total += fix_land[p, d - 1, 64:80].astype(F32)
        fix[p, RANK + 64 : RANK + 80] = total.astype(BF16)
        fixes = Group(fix_land.at[p, 0, 80:96])
        fixes.send(fix.at[p, RANK + 64 : RANK + 80], fix_land.at[p, 0, 80:96], twin_dev)
        twins.take()
        fixes.take()

    def fetch(p, coord, owner):
        def choose(j):
            place = owner[coords[coord, wide * DEPTH + j]]
            spot = (place // 8, (place // 2) % SIDE, place % CORES)
            for h in range(2):
                zsend[p, j, 2 * h : 2 * h + 2] = gath[p, h, spot[0], spot[1], spot[2]].reshape(
                    2, 16, RANK
                )

        fetched = Group(kbuf.at[p, :, 0:7])
        for d in around:
            choose(z_at(d))
            fetched.send(zsend.at[p, z_at(d)], kbuf.at[p, :, z], z_dev(d))
        choose(z)
        kbuf[p, :, z] = zsend[p, z]
        return fetched

    def gram_start(p):
        total = jnp.zeros((RANK, RANK), F32)
        for h in range(2):
            for a in range(SIDE):
                some = gath[p, h, a].reshape(SIDE * CORES * 32, RANK)
                total += lax.dot_general(
                    some, some, (((0,), (0,)), ((), ())), preferred_element_type=F32
                )
        gpart[p] = total
        own = lines(wide, 8)
        both = fix[p, RANK + 64 : RANK + 80].astype(F32) + fix_land[p, 0, 80:96].astype(F32)
        gpart[p, own] += jnp.where(c == 0, both[0:8], both[8:16])
        group = Group(gland.at[p, 0:7])
        for d in around:
            group.send(gpart.at[p, own], gland.at[p, z], z_dev(d))
        gland[p, z] = gpart[p, own]
        return group

    def gram_sum(p, group):
        group.take()
        gfull[p, x, y, c] = jnp.sum(gland[p], axis=0)
        spot = gfull.at[p, x, y, c]
        group = Group(gfull.at[p, 0, 0:3, 0])
        for d in (2, 1, 3):
            group.send(spot, spot, x_dev(d))
        return group

    def gram_line(p, group):
        group.take()
        line = gfull.at[p, :, y, c]
        group = Group(gfull.at[p, 0:3, :, 0])
        for d in (2, 1, 3):
            group.send(line, line, y_dev(d))
        return group

    def gram_plane(p, group):
        group.take()
        plane = gfull.at[p, :, :, c]
        group = Group(gfull.at[p, :, :, 0])
        group.send(plane, plane, twin_dev)
        return group

    def inverse_start(p, group):
        group.take()
        gram = gfull[p].reshape(RANK, RANK) * time_gram
        penalty = jnp.sum(gram * eye) / RANK
        base[...] = gram / penalty + eye
        t = SCALES[0]
        gain = 2.0 * t * t / (2.0 * t * t - 1.0)
        approx[...] = (eye * 2.0 - base[...] * (1.0 / 129.0)) * (gain / 129.0)
        return penalty

    def inverse_steps(first, last):
        def step(_, t):
            t2 = 2.0 * t * t - 1.0
            now = approx[...]
            error = eye - exact_dot(base[...], now)
            approx[...] = (now + exact_dot(now, error)) * ((t2 + 1.0) / t2)
            return t2

        lax.fori_loop(first, last, step, F32(SCALES[first + 1]))

    def tile_half(p, h, forward, khatri_t):
        total = jnp.zeros((BLOCK // 2, RANK), F32)
        cut = slice(h * 256, (h + 1) * 256)
        for k in range(TIMES):
            if forward:
                total += jnp.dot(act[k, cut, :], khatri[k], preferred_element_type=F32)
            else:
                total += jnp.dot(khatri_t[k], act[k, :, cut], preferred_element_type=F32)
        if not forward:
            total = total.T
        partial[p, 2 * h : 2 * h + 2] = total.reshape(2, DEPTH, 16, RANK)
        pair = pl.ds(2 * h, 2)
        group = Group(tland.at[p, h, 0:7])
        for d in around:
            group.send(partial.at[p, pair, z_at(d)], tland.at[p, h, z], z_dev(d))
        tland[p, h, z] = partial[p, 2 * h : 2 * h + 2, z]
        return group

    def reduced(p, coord, owner, arrived, gram):
        targets = [owner[coords[coord, wide * DEPTH + j]] for j in range(DEPTH)]
        twin_targets = [owner[coords[coord, twin * DEPTH + j]] for j in range(DEPTH)]

        def pass_on(h):
            arrived[h].take()
            twins = Group(cland.at[p, h])
            twins.send(tland.at[p, h], cland.at[p, h], twin_dev)
            return twins

        def spread(h, twins):
            twins.take()
            firsts = [Group(first_land.at[p, h, v]) for v in range(2)]
            for d in (2, 1, 3, 0):
                for v in range(2):
                    a = lax.rem((x, y)[v] + d, SIDE)
                    cut = slice(v * 128, (v + 1) * 128)

                    def place(b, carry):
                        block = ((a * SIDE + b) if v == 0 else (b * SIDE + a)) * CORES + c
                        total = jnp.zeros((2, 16, 128), F32)
                        for j in range(DEPTH):
                            total += tland[p, h, j, :, :, cut] * (targets[j] == block).astype(F32)
                            total += cland[p, h, j, :, :, cut] * (
                                twin_targets[j] == block
                            ).astype(F32)
                        dense[p, h, v, a, b] = total
                        return carry

                    lax.fori_loop(0, SIDE, place, 0)
                    if d:
                        firsts[v].send(
                            dense.at[p, h, v, a],
                            first_land.at[p, h, v, d - 1],
                            (x_dev, y_dev)[v](d),
                        )
            return firsts

        def spread_on(h, firsts):
            seconds = [Group(last_land.at[p, h, v]) for v in range(2)]
            for v in range(2):
                firsts[v].take()
                middle[p, h, v] = (dense[p, h, v, (x, y)[v]] + first_land[p, h, v, 0]) + (
                    first_land[p, h, v, 1] + first_land[p, h, v, 2]
                )
                for d in (2, 1, 3):
                    seconds[v].send(
                        middle.at[p, h, v, lax.rem((y, x)[v] + d, SIDE)],
                        last_land.at[p, h, v, d - 1],
                        (y_dev, x_dev)[v](d),
                    )
            return seconds

        def finish(h, seconds):
            parts = []
            for v in range(2):
                seconds[v].take()
                total = (middle[p, h, v, (y, x)[v]] + last_land[p, h, v, 0]) + (
                    last_land[p, h, v, 1] + last_land[p, h, v, 2]
                )
                parts.append(total.reshape(32, 128))
            return jnp.concatenate(parts, axis=1)

        gram = gram_sum(p, gram)
        twins = [pass_on(0)]
        gram = gram_line(p, gram)
        firsts = [spread(0, twins[0])]
        gram = gram_plane(p, gram)
        penalty = inverse_start(p, gram)
        inverse_steps(0, 2)
        twins.append(pass_on(1))
        seconds = [spread_on(0, firsts[0])]
        firsts.append(spread(1, twins[1]))
        inverse_steps(2, 5)
        seconds.append(spread_on(1, firsts[1]))
        inverse_steps(5, STEPS)
        return jnp.concatenate([finish(h, seconds[h]) for h in range(2)], axis=0), penalty

    def admm(sums, factor, dual, penalty):
        inverse = approx[...]
        for _ in range(PASSES):
            target = exact_dot(sums + penalty * (factor + dual), inverse) / penalty
            factor = jnp.maximum(target - dual, 0.0)
            dual = dual + factor - target
        return factor, dual

    def give_back(p, factor, dual):
        for a, rows in ((0, factor), (1, dual)):
            for n in range(DEPTH):
                opack[p, n, a] = jnp.concatenate(
                    [
                        rows[t * 16 : (t + 1) * 16, n * 32 : (n + 1) * 32]
                        for t in range(4)
                    ],
                    axis=1,
                )
        group = Group(oland.at[p, :, 0:7])
        for d in around:
            group.send(opack.at[p, z_at(d)], oland.at[p, :, z], z_dev(d))
        oland[p, :, z] = opack[p, z]
        return group

    def take_back(p, group, outs):
        group.take()
        for a in range(2):
            turned = oland[p, a].reshape(128, 128).T
            for t in range(4):
                outs[a][:, t * 128 : (t + 1) * 128] = turned[t * 32 : (t + 1) * 32, :]

    def update(p, rows, factor_at, dual_at, own_coord, own, other, after_start, after_middle, after_gram):
        forward = p == 0
        gather(p, rows, after_start, after_middle)
        fetched = fetch(p, 1 - own_coord, other)
        gram = gram_start(p)
        after_gram()
        fetched.take()
        if forward:
            loads[8].wait()
        low = kbuf[p].reshape(BLOCK, RANK).astype(F32)
        khatri_t = None
        if forward:
            for k in range(TIMES):
                khatri[k] = (low * times[k : k + 1, :]).astype(BF16)
        else:
            turned = low.T
            columns = times.T
            khatri_t = [(turned * columns[:, k : k + 1]).astype(BF16) for k in range(TIMES)]
        arrived = [tile_half(p, h, forward, khatri_t) for h in range(2)]
        sums, penalty = reduced(p, own_coord, own, arrived, gram)
        return admm(sums, held[factor_at], held[dual_at], penalty)

    nothing = lambda: None
    users, user_duals = update(
        0, held[0], 2, 3, 0, user_owner, item_owner, send_rest, unpack_rest, nothing
    )
    returned = []
    items, item_duals = update(
        1,
        users,
        0,
        1,
        1,
        item_owner,
        user_owner,
        nothing,
        lambda: returned.append(give_back(0, users, user_duals)),
        lambda: take_back(0, returned[0], (out_users, out_user_duals)),
    )
    take_back(1, give_back(1, items, item_duals), (out_items, out_item_duals))
    for group in groups:
        group.whole.wait_send()


def settle_kernel(*refs):
    for a in range(4):
        refs[4 + a][...] = refs[a][...]


def local(
    activity,
    tile_coords,
    user_owner,
    item_owner,
    user_factor,
    item_factor,
    time_factor,
    user_dual,
    item_dual,
):
    hbm = pl.BlockSpec(memory_space=pltpu.HBM)
    vmem = pl.BlockSpec(memory_space=pltpu.VMEM)
    slab = jax.ShapeDtypeStruct((RANK // DEPTH, BLOCK), F32)
    outs = pl.pallas_call(
        sweep_kernel,
        out_shape=(slab,) * 4,
        in_specs=[hbm] * 9,
        out_specs=(vmem,) * 4,
        scratch_shapes=[
            pltpu.VMEM((TIMES, BLOCK, BLOCK), BF16),
            pltpu.SMEM((2, RANK), jnp.int32),
            pltpu.SMEM((32,), jnp.int32),
            pltpu.SMEM((32,), jnp.int32),
            pltpu.VMEM((4, RANK // DEPTH, BLOCK), F32),
            pltpu.VMEM((TIMES, RANK), F32),
            pltpu.VMEM((4, 128, 128), F32),
            pltpu.VMEM((4, DEPTH, 16, 128), F32),
            pltpu.VMEM((4, 64, RANK), F32),
            pltpu.VMEM((TIMES, BLOCK, RANK), BF16),
            pltpu.VMEM((2, 2, SIDE, SIDE, CORES, 32, RANK), BF16),
            pltpu.VMEM((2, DEPTH, 4, 16, RANK), BF16),
            pltpu.VMEM((2, 4, DEPTH, 16, RANK), BF16),
            pltpu.VMEM((2, RANK, RANK), F32),
            pltpu.VMEM((2, RANK + 80, RANK), BF16),
            pltpu.VMEM((2, SIDE - 1, 96, RANK), BF16),
            pltpu.VMEM((2, DEPTH, 8, RANK), F32),
            pltpu.VMEM((2, SIDE, SIDE, CORES, 8, RANK), F32),
            pltpu.VMEM((RANK, RANK), F32),
            pltpu.VMEM((RANK, RANK), F32),
            pltpu.VMEM((2, 4, DEPTH, 16, RANK), F32),
            pltpu.VMEM((2, 2, DEPTH, 2, 16, RANK), F32),
            pltpu.VMEM((2, 2, DEPTH, 2, 16, RANK), F32),
            pltpu.VMEM((2, 2, 2, SIDE, SIDE, 2, 16, 128), F32),
            pltpu.VMEM((2, 2, 2, SIDE - 1, SIDE, 2, 16, 128), F32),
            pltpu.VMEM((2, 2, 2, SIDE, 2, 16, 128), F32),
            pltpu.VMEM((2, 2, 2, SIDE - 1, 2, 16, 128), F32),
            pltpu.VMEM((2, DEPTH, 2, 16, 128), F32),
            pltpu.VMEM((2, 2, DEPTH, 16, 128), F32),
            pltpu.SemaphoreType.DMA((SEMS,)),
            pltpu.SemaphoreType.DMA((9,)),
        ],
        compiler_params=pltpu.CompilerParams(
            collective_id=0, has_side_effects=True, vmem_limit_bytes=56 * 2**20
        ),
        name="sweep",
    )(
        activity,
        tile_coords.T,
        user_owner,
        item_owner,
        user_factor.T,
        item_factor.T,
        time_factor,
        user_dual.T,
        item_dual.T,
    )
    outs = pl.pallas_call(settle_kernel, out_shape=(slab,) * 4, name="settle")(*outs)
    users, items, user_duals, item_duals = (out.T for out in outs)
    return (users, items, user_duals, item_duals)


def solution(mesh):
    split = Mesh(
        mesh.devices.reshape(SIDE, SIDE, CORES, mesh.shape["narrow"]),
        WIDE_NARROW,
    )
    in_specs = (
        P(WIDE_NARROW, None, None, None),
        P(),
        P(),
        P(),
        P(WIDE, "narrow"),
        P(WIDE, "narrow"),
        P(),
        P(WIDE, "narrow"),
        P(WIDE, "narrow"),
    )
    out_specs = (P(WIDE, "narrow"), P(WIDE, "narrow"), P(WIDE, "narrow"), P(WIDE, "narrow"))
    return jax.shard_map(local, mesh=split, in_specs=in_specs, out_specs=out_specs, check_vma=False)
```

time: 142 us -> 116 us (0.82)
  Pallas kernels: 130 us -> 115 us
  local copies, waits for them, and re-layouts: 10.7 us -> 0 us
    pallas_call x1 -> x2, Pallas kernels: 130 us -> 115 us  [the longest x1 113 us: local(): pl.pallas_call(sweep_kernel, out_shape=(slab,) * 4, in_specs=[hbm] * 9, o...]
    unnamed x22 -> x0, local copies, waits for them, and re-layouts: 10.7 us -> none
where the time goes in v1:
time: 116 us; the launch traced here: 115 us
  Pallas kernels  115 us (99%)
    pallas_call x1, Pallas kernels, local(): pl.pallas_call(sweep_kernel, out_shape=(slab,) * 4, in_specs=[hbm] * 9, o...  113 us

profile of v1, /device:TPU:1, one launch (start us, length us, event | category | flops | bytes accessed | tf_op | source)
XLA Modules:
  0.0 115.4 jit_solution(2552440460267553833)
XLA Ops:
  0.6 113.1 %sweep.1 = (f32[32,512]{1,0:T(8,128)}, f32[32,512]{1,0:T(8,128)}, f32[32,512]{1,0:T(8,128)}, f32[32,512]{1,0:T(8,128)}) custom-call(bf16[1,8,512,512]{3,2,1,0:T(8,128)(2,1)} %act_hbm.1, s32[2,256]{1,0:T(2,128)} %bitcast.13, s32[32]{0:T(128)} %user_owner_hbm.1, s32[32]{0:T(128)} %item_owner_hbm.1, f32[32,512]{1,0:T(8,128)} %bitcast.9, f32[32,512]{1,0:T(8,128)} %bitcast.10, ...), custom_call_target="tpu_custom_call" | custom-call | tf_op jit(solution)/shard_map/sweep/pallas_call | solution.py:519
  113.7 1.6 %settle.1 = (f32[32,512]{1,0:T(8,128)}, f32[32,512]{1,0:T(8,128)}, f32[32,512]{1,0:T(8,128)}, f32[32,512]{1,0:T(8,128)}) custom-call(f32[32,512]{1,0:T(8,128)} %get-tuple-element.12.refs_0_, f32[32,512]{1,0:T(8,128)} %get-tuple-element.13.refs_1_, f32[32,512]{1,0:T(8,128)} %get-tuple-element.14.refs_2_, f32[32,512]{1,0:T(8,128)} %get-tuple-element.15.refs_3_), custom_call_target="tpu_custom_call" | custom-call | tf_op jit(solution)/shard_map/settle/pallas_call | solution.py:572

commit v2 on v1

--- a/solution.py
+++ b/solution.py
@@ -13,7 +13,7 @@
 SIDE = 4
 CORES = 2
 DEPTH = 8
-STEPS = 7
+STEPS = 6
 SCALES = [129.0 / 128.0]
 for _ in range(STEPS):
     SCALES.append(2.0 * SCALES[-1] ** 2 - 1.0)
@@ -57,6 +57,9 @@
     zsend,
     kbuf,
     gpart,
+    xland,
+    yland,
+    high_part,
     fix,
     fix_land,
     gland,
@@ -158,47 +161,106 @@
             )
 
     loads[0].wait()
-    pack(0)
     pl.semaphore_wait(barrier, len(peers))
-    lead = Group(landed.at[0, 0:7])
-    for d in around:
-        lead.send(packed.at[0, lines(z_at(d), 16)], landed.at[0, z], z_dev(d))
-    landed[0, z] = packed[0, lines(z, 16)]
-    for load in loads[1:8]:
-        load.wait()
-    for a in (1, 2, 3):
-        pack(a)
-        landed[a, z] = packed[a, lines(z, 16)]
-    times = time_factor[...]
-    time_gram = exact_dot(times.T, times)
-    eye = (
-        lax.broadcasted_iota(jnp.int32, (RANK, RANK), 0)
-        == lax.broadcasted_iota(jnp.int32, (RANK, RANK), 1)
-    ).astype(F32)
-    lead.take()
-    unpack(0)
-
-    rest = Group(landed.at[1:4, 0:7])
-
-    def send_rest():
+
+    rows_group = Group(landed.at[:, 0:7])
+
+    def send_rows():
+        for load in loads[1:8]:
+            load.wait()
+        for a in range(4):
+            pack(a)
+            landed[a, z] = packed[a, lines(z, 16)]
         for d in around:
-            rest.send(
-                packed.at[1:4, lines(z_at(d), 16)], landed.at[1:4, z], z_dev(d)
+            rows_group.send(packed.at[:, lines(z_at(d), 16)], landed.at[:, z], z_dev(d))
+
+    def take_rows():
+        rows_group.take()
+        for a in range(4):
+            unpack(a)
+
+    def gather(p, halves, after_start, after_middle, after_plane):
+        buf = gath.at[p]
+        own = (buf.at[0, c, y, x], buf.at[1, c, x, y])
+        for h in range(2):
+            own[h][...] = halves[h].astype(BF16)
+        starts = Group(buf.at[0, 0, 0:2, 0:3])
+        for d in (2, 1, 3):
+            for h in range(2):
+                starts.send(own[h], own[h], (x_dev, y_dev)[h](d))
+        after_start()
+        starts.take()
+        middles = Group(buf.at[:, 0, 0:3])
+        mine = (buf.at[0, c, y], buf.at[1, c, x])
+        for d in (2, 1, 3):
+            for h in range(2):
+                middles.send(mine[h], mine[h], (y_dev, x_dev)[h](d))
+        after_middle()
+        middles.take()
+        twins = Group(buf.at[:, 0])
+        for h in range(2):
+            twins.send(buf.at[h, c], buf.at[h, c], twin_dev)
+        after_plane()
+        twins.take()
+
+    def fetch(p, coord, owner):
+        def choose(j):
+            place = owner[coords[coord, wide * DEPTH + j]]
+            a, b, core = place // 8, (place // 2) % SIDE, place % CORES
+            zsend[p, j, 0:2] = gath[p, 0, core, b, a].reshape(2, 16, RANK)
+            zsend[p, j, 2:4] = gath[p, 1, core, a, b].reshape(2, 16, RANK)
+
+        fetched = Group(kbuf.at[p, 0:7])
+        for d in around:
+            choose(z_at(d))
+            fetched.send(zsend.at[p, z_at(d)], kbuf.at[p, z], z_dev(d))
+        choose(z)
+        kbuf[p, z] = zsend[p, z]
+        return fetched
+
+    def gram_local(p, rows):
+        gpart[p, 0:RANK] = exact_dot(rows.T, rows)
+
+    def gram_x(p):
+        group = Group(xland.at[p])
+        for d in (2, 1, 3):
+            group.send(
+                gpart.at[p, lines(lax.rem(x + d, SIDE), 64)], xland.at[p, d - 1], x_dev(d)
             )
-
-    def unpack_rest():
-        rest.take()
-        for a in (1, 2, 3):
-            unpack(a)
-
-    def gather(p, rows, after_start, after_middle):
-        buf = gath.at[p]
-        for h in range(2):
-            buf[h, x, y, c] = rows[h * 32 : (h + 1) * 32].astype(BF16)
-        starts = Group(buf.at[0, 0, 0:3])
-        for d in (2, 1, 3):
-            for h in range(2):
-                starts.send(buf.at[h, x, y, c], buf.at[h, x, y, c], (x_dev, y_dev)[h](d))
+        return group
+
+    def gram_y(p, group):
+        group.take()
+        gpart[p, RANK : RANK + 64] = (gpart[p, lines(x, 64)] + xland[p, 0]) + (
+            xland[p, 1] + xland[p, 2]
+        )
+        group = Group(yland.at[p, 0:3])
+        for d in (2, 1, 3):
+            group.send(
+                gpart.at[p, lines(lax.rem(y + d, SIDE) + 16, 16)], yland.at[p, d - 1], y_dev(d)
+            )
+        return group
+
+    def gram_twin(p, group):
+        group.take()
+        gpart[p, RANK + 64 : RANK + 80] = (gpart[p, lines(y + 16, 16)] + yland[p, 0]) + (
+            yland[p, 1] + yland[p, 2]
+        )
+        group = Group(yland.at[p, 3])
+        group.send(gpart.at[p, RANK + 64 : RANK + 80], yland.at[p, 3], twin_dev)
+        return group
+
+    def gram_z(p, group):
+        group.take()
+        both = gpart[p, RANK + 64 : RANK + 80] + yland[p, 3]
+        gpart[p, RANK + 80 : RANK + 88] = jnp.where(c == 0, both[0:8], both[8:16])
+        group = Group(gland.at[p, 0:7])
+        for d in around:
+            group.send(gpart.at[p, RANK + 80 : RANK + 88], gland.at[p, z], z_dev(d))
+        gland[p, z] = gpart[p, RANK + 80 : RANK + 88]
+        return group
+
+    def fix_local(rows):
         high = rows.astype(BF16)
         low = rows - high.astype(F32)
         missed = lax.dot_general(
@@ -207,108 +269,85 @@
             (((0,), (0,)), ((), ())),
             preferred_element_type=F32,
         )
-        fix[p, 0:RANK] = (missed + missed.T).astype(BF16)
-        fixes = Group(fix_land.at[p, :, 0:64])
-        for d in (2, 1, 3):
-            fixes.send(
-                fix.at[p, lines(lax.rem(x + d, SIDE), 64)], fix_land.at[p, d - 1, 0:64], x_dev(d)
+        fix[0:RANK] = (missed + missed.T).astype(BF16)
+
+    def fix_x():
+        group = Group(fix_land.at[:, 0:64])
+        for d in (2, 1, 3):
+            group.send(
+                fix.at[lines(lax.rem(x + d, SIDE), 64)], fix_land.at[d - 1, 0:64], x_dev(d)
             )
-        after_start()
-        starts.take()
-        middles = Group(buf.at[0, 0:3])
-        mine = (buf.at[0, :, y, c], buf.at[1, x, :, c])
-        for d in (2, 1, 3):
-            for h in range(2):
-                middles.send(mine[h], mine[h], (y_dev, x_dev)[h](d))
-        fixes.take()
-        total = fix[p, lines(x, 64)].astype(F32)
+        return group
+
+    def fix_y(group):
+        group.take()
+        total = fix[lines(x, 64)].astype(F32)
         for d in (1, 2, 3):
-            total += fix_land[p, d - 1, 0:64].astype(F32)
-        fix[p, RANK : RANK + 64] = total.astype(BF16)
-        fixes = Group(fix_land.at[p, :, 64:80])
-        for d in (2, 1, 3):
-            fixes.send(
-                fix.at[p, lines(lax.rem(y + d, SIDE) + 16, 16)],
-                fix_land.at[p, d - 1, 64:80],
-                y_dev(d),
+            total += fix_land[d - 1, 0:64].astype(F32)
+        fix[RANK : RANK + 64] = total.astype(BF16)
+        group = Group(fix_land.at[:, 64:80])
+        for d in (2, 1, 3):
+            group.send(
+                fix.at[lines(lax.rem(y + d, SIDE) + 16, 16)], fix_land.at[d - 1, 64:80], y_dev(d)
             )
-        after_middle()
-        middles.take()
-        twins = Group(buf.at[:, :, :, 0])
-        for h in range(2):
-            twins.send(buf.at[h, :, :, c], buf.at[h, :, :, c], twin_dev)
-        fixes.take()
-        total = fix[p, lines(y + 16, 16)].astype(F32)
+        return group
+
+    def fix_twin(group):
+        group.take()
+        total = fix[lines(y + 16, 16)].astype(F32)
         for d in (1, 2, 3):
-            total += fix_land[p, d - 1, 64:80].astype(F32)
-        fix[p, RANK + 64 : RANK + 80] = total.astype(BF16)
-        fixes = Group(fix_land.at[p, 0, 80:96])
-        fixes.send(fix.at[p, RANK + 64 : RANK + 80], fix_land.at[p, 0, 80:96], twin_dev)
-        twins.take()
-        fixes.take()
-
-    def fetch(p, coord, owner):
-        def choose(j):
-            place = owner[coords[coord, wide * DEPTH + j]]
-            spot = (place // 8, (place // 2) % SIDE, place % CORES)
-            for h in range(2):
-                zsend[p, j, 2 * h : 2 * h + 2] = gath[p, h, spot[0], spot[1], spot[2]].reshape(
-                    2, 16, RANK
-                )
-
-        fetched = Group(kbuf.at[p, :, 0:7])
-        for d in around:
-            choose(z_at(d))
-            fetched.send(zsend.at[p, z_at(d)], kbuf.at[p, :, z], z_dev(d))
-        choose(z)
-        kbuf[p, :, z] = zsend[p, z]
-        return fetched
-
-    def gram_start(p):
+            total += fix_land[d - 1, 64:80].astype(F32)
+        fix[RANK + 64 : RANK + 80] = total.astype(BF16)
+        group = Group(fix_land.at[0, 80:96])
+        group.send(fix.at[RANK + 64 : RANK + 80], fix_land.at[0, 80:96], twin_dev)
+        return group
+
+    def gram_high(p, group):
         total = jnp.zeros((RANK, RANK), F32)
         for h in range(2):
             for a in range(SIDE):
-                some = gath[p, h, a].reshape(SIDE * CORES * 32, RANK)
+                some = gath[p, h, a // 2, (a % 2) * 2 : (a % 2) * 2 + 2].reshape(256, RANK)
                 total += lax.dot_general(
                     some, some, (((0,), (0,)), ((), ())), preferred_element_type=F32
                 )
-        gpart[p] = total
+        high_part[...] = total
+        group.take()
         own = lines(wide, 8)
-        both = fix[p, RANK + 64 : RANK + 80].astype(F32) + fix_land[p, 0, 80:96].astype(F32)
-        gpart[p, own] += jnp.where(c == 0, both[0:8], both[8:16])
+        both = fix[RANK + 64 : RANK + 80].astype(F32) + fix_land[0, 80:96].astype(F32)
+        high_part[own] += jnp.where(c == 0, both[0:8], both[8:16])
         group = Group(gland.at[p, 0:7])
         for d in around:
-            group.send(gpart.at[p, own], gland.at[p, z], z_dev(d))
-        gland[p, z] = gpart[p, own]
+            group.send(high_part.at[own], gland.at[p, z], z_dev(d))
+        gland[p, z] = high_part[own]
         return group
 
     def gram_sum(p, group):
         group.take()
-        gfull[p, x, y, c] = jnp.sum(gland[p], axis=0)
-        spot = gfull.at[p, x, y, c]
-        group = Group(gfull.at[p, 0, 0:3, 0])
+        spot = gfull.at[p, c, y, x]
+        spot[...] = jnp.sum(gland[p], axis=0)
+        group = Group(gfull.at[p, 0, 0, 0:3])
         for d in (2, 1, 3):
             group.send(spot, spot, x_dev(d))
         return group
 
     def gram_line(p, group):
         group.take()
-        line = gfull.at[p, :, y, c]
-        group = Group(gfull.at[p, 0:3, :, 0])
+        line = gfull.at[p, c, y]
+        group = Group(gfull.at[p, 0, 0:3])
         for d in (2, 1, 3):
             group.send(line, line, y_dev(d))
         return group
 
     def gram_plane(p, group):
         group.take()
-        plane = gfull.at[p, :, :, c]
-        group = Group(gfull.at[p, :, :, 0])
+        plane = gfull.at[p, c]
+        group = Group(gfull.at[p, 0])
         group.send(plane, plane, twin_dev)
         return group
 
     def inverse_start(p, group):
         group.take()
-        gram = gfull[p].reshape(RANK, RANK) * time_gram
+        gram = gfull[p].transpose(2, 1, 0, 3, 4).reshape(RANK, RANK) * time_gram
         penalty = jnp.sum(gram * eye) / RANK
         base[...] = gram / penalty + eye
         t = SCALES[0]
@@ -316,12 +355,25 @@
         approx[...] = (eye * 2.0 - base[...] * (1.0 / 129.0)) * (gain / 129.0)
         return penalty
 
+    def split(a):
+        high = a.astype(BF16)
+        return high, (a - high.astype(F32)).astype(BF16)
+
+    def near_dot(a, b):
+        (ah, al), (bh, bl) = split(a), split(b)
+        return (
+            jnp.dot(ah, bl, preferred_element_type=F32)
+            + jnp.dot(al, bh, preferred_element_type=F32)
+        ) + jnp.dot(ah, bh, preferred_element_type=F32)
+
     def inverse_steps(first, last):
+        dot = near_dot if last < STEPS else exact_dot
+
         def step(_, t):
             t2 = 2.0 * t * t - 1.0
             now = approx[...]
-            error = eye - exact_dot(base[...], now)
-            approx[...] = (now + exact_dot(now, error)) * ((t2 + 1.0) / t2)
+            error = eye - dot(base[...], now)
+            approx[...] = (now + dot(now, error)) * ((t2 + 1.0) / t2)
             return t2
 
         lax.fori_loop(first, last, step, F32(SCALES[first + 1]))
@@ -336,12 +388,11 @@
                 total += jnp.dot(khatri_t[k], act[k, :, cut], preferred_element_type=F32)
         if not forward:
             total = total.T
-        partial[p, 2 * h : 2 * h + 2] = total.reshape(2, DEPTH, 16, RANK)
-        pair = pl.ds(2 * h, 2)
+        partial[p, h] = total.reshape(2, DEPTH, 16, RANK).swapaxes(0, 1)
         group = Group(tland.at[p, h, 0:7])
         for d in around:
-            group.send(partial.at[p, pair, z_at(d)], tland.at[p, h, z], z_dev(d))
-        tland[p, h, z] = partial[p, 2 * h : 2 * h + 2, z]
+            group.send(partial.at[p, h, z_at(d)], tland.at[p, h, z], z_dev(d))
+        tland[p, h, z] = partial[p, h, z]
         return group
 
     def reduced(p, coord, owner, arrived, gram):
@@ -416,10 +467,11 @@
         inverse_steps(0, 2)
         twins.append(pass_on(1))
         seconds = [spread_on(0, firsts[0])]
+        inverse_steps(2, 3)
         firsts.append(spread(1, twins[1]))
-        inverse_steps(2, 5)
+        inverse_steps(3, 4)
         seconds.append(spread_on(1, firsts[1]))
-        inverse_steps(5, STEPS)
+        inverse_steps(4, STEPS)
         return jnp.concatenate([finish(h, seconds[h]) for h in range(2)], axis=0), penalty
 
     def admm(sums, factor, dual, penalty):
@@ -453,45 +505,65 @@
             for t in range(4):
                 outs[a][:, t * 128 : (t + 1) * 128] = turned[t * 32 : (t + 1) * 32, :]
 
-    def update(p, rows, factor_at, dual_at, own_coord, own, other, after_start, after_middle, after_gram):
-        forward = p == 0
-        gather(p, rows, after_start, after_middle)
-        fetched = fetch(p, 1 - own_coord, other)
-        gram = gram_start(p)
-        after_gram()
-        fetched.take()
-        if forward:
-            loads[8].wait()
-        low = kbuf[p].reshape(BLOCK, RANK).astype(F32)
-        khatri_t = None
-        if forward:
+    nothing = lambda: None
+
+    def table(p, low):
+        if p == 0:
             for k in range(TIMES):
                 khatri[k] = (low * times[k : k + 1, :]).astype(BF16)
-        else:
-            turned = low.T
-            columns = times.T
-            khatri_t = [(turned * columns[:, k : k + 1]).astype(BF16) for k in range(TIMES)]
-        arrived = [tile_half(p, h, forward, khatri_t) for h in range(2)]
-        sums, penalty = reduced(p, own_coord, own, arrived, gram)
-        return admm(sums, held[factor_at], held[dual_at], penalty)
-
-    nothing = lambda: None
-    users, user_duals = update(
-        0, held[0], 2, 3, 0, user_owner, item_owner, send_rest, unpack_rest, nothing
+            return None
+        turned = low.T
+        columns = times.T
+        return [(turned * columns[:, k : k + 1]).astype(BF16) for k in range(TIMES)]
+
+    gather(
+        0,
+        [slabs[0, :, 0:256], slabs[0, :, 256:512]],
+        nothing,
+        send_rows,
+        nothing,
     )
+    fetched = fetch(0, 1, item_owner)
+    times = time_factor[...]
+    time_gram = exact_dot(times.T, times)
+    eye = (
+        lax.broadcasted_iota(jnp.int32, (RANK, RANK), 0)
+        == lax.broadcasted_iota(jnp.int32, (RANK, RANK), 1)
+    ).astype(F32)
+    take_rows()
+    gram_local(0, held[0])
+    gram = gram_twin(0, gram_y(0, gram_x(0)))
+    fetched.take()
+    loads[8].wait()
+    turned = jnp.concatenate(
+        [kbuf[0, :, 2 * h : 2 * h + 2].reshape(RANK, 256) for h in range(2)], axis=1
+    )
+    table(0, turned.astype(F32).T)
+    gram = gram_z(0, gram)
+    arrived = [tile_half(0, h, True, None) for h in range(2)]
+    sums, penalty = reduced(0, 0, user_owner, arrived, gram)
+    users, user_duals = admm(sums, held[2], held[3], penalty)
+
     returned = []
-    items, item_duals = update(
+    grams = []
+    gather(
         1,
-        users,
-        0,
-        1,
-        1,
-        item_owner,
-        user_owner,
-        nothing,
-        lambda: returned.append(give_back(0, users, user_duals)),
-        lambda: take_back(0, returned[0], (out_users, out_user_duals)),
+        [users[0:32], users[32:64]],
+        lambda: (fix_local(users), grams.append(fix_x())),
+        lambda: (
+            grams.append(fix_y(grams[0])),
+            returned.append(give_back(0, users, user_duals)),
+        ),
+        lambda: grams.append(fix_twin(grams[1])),
     )
+    fetched = fetch(1, 0, user_owner)
+    gram = gram_high(1, grams[2])
+    take_back(0, returned[0], (out_users, out_user_duals))
+    fetched.take()
+    khatri_t = table(1, kbuf[1].swapaxes(0, 1).reshape(BLOCK, RANK).astype(F32))
+    arrived = [tile_half(1, h, False, khatri_t) for h in range(2)]
+    sums, penalty = reduced(1, 1, item_owner, arrived, gram)
+    items, item_duals = admm(sums, held[0], held[1], penalty)
     take_back(1, give_back(1, items, item_duals), (out_items, out_item_duals))
     for group in groups:
         group.whole.wait_send()
@@ -532,17 +604,20 @@
             pltpu.VMEM((4, DEPTH, 16, 128), F32),
             pltpu.VMEM((4, 64, RANK), F32),
             pltpu.VMEM((TIMES, BLOCK, RANK), BF16),
-            pltpu.VMEM((2, 2, SIDE, SIDE, CORES, 32, RANK), BF16),
+            pltpu.VMEM((2, 2, CORES, SIDE, SIDE, 32, RANK), BF16),
             pltpu.VMEM((2, DEPTH, 4, 16, RANK), BF16),
-            pltpu.VMEM((2, 4, DEPTH, 16, RANK), BF16),
-            pltpu.VMEM((2, RANK, RANK), F32),
-            pltpu.VMEM((2, RANK + 80, RANK), BF16),
-            pltpu.VMEM((2, SIDE - 1, 96, RANK), BF16),
+            pltpu.VMEM((2, DEPTH, 4, 16, RANK), BF16),
+            pltpu.VMEM((1, RANK + 88, RANK), F32),
+            pltpu.VMEM((1, SIDE - 1, 64, RANK), F32),
+            pltpu.VMEM((1, SIDE, 16, RANK), F32),
+            pltpu.VMEM((RANK, RANK), F32),
+            pltpu.VMEM((RANK + 80, RANK), BF16),
+            pltpu.VMEM((SIDE - 1, 96, RANK), BF16),
             pltpu.VMEM((2, DEPTH, 8, RANK), F32),
-            pltpu.VMEM((2, SIDE, SIDE, CORES, 8, RANK), F32),
+            pltpu.VMEM((2, CORES, SIDE, SIDE, 8, RANK), F32),
             pltpu.VMEM((RANK, RANK), F32),
             pltpu.VMEM((RANK, RANK), F32),
-            pltpu.VMEM((2, 4, DEPTH, 16, RANK), F32),
+            pltpu.VMEM((2, 2, DEPTH, 2, 16, RANK), F32),
             pltpu.VMEM((2, 2, DEPTH, 2, 16, RANK), F32),
             pltpu.VMEM((2, 2, DEPTH, 2, 16, RANK), F32),
             pltpu.VMEM((2, 2, 2, SIDE, SIDE, 2, 16, 128), F32),

time: 116 us -> 113 us (0.974)
  Pallas kernels: 115 us -> 112 us
    pallas_call x1, Pallas kernels: 113 us -> 111 us  [local(): pl.pallas_call(sweep_kernel, out_shape=(slab,) * 4, in_specs=[hbm] * 9, o...]
where the time goes in v2:
time: 113 us
  Pallas kernels  112 us (99%)
    pallas_call x1, Pallas kernels, local(): pl.pallas_call(sweep_kernel, out_shape=(slab,) * 4, in_specs=[hbm] * 9, o...  111 us

profile of v2, /device:TPU:1, one launch (start us, length us, event | category | flops | bytes accessed | tf_op | source)
XLA Modules:
  0.0 112.9 jit_solution(10360122044534400619)
XLA Ops:
  0.6 110.6 %sweep.1 = (f32[32,512]{1,0:T(8,128)}, f32[32,512]{1,0:T(8,128)}, f32[32,512]{1,0:T(8,128)}, f32[32,512]{1,0:T(8,128)}) custom-call(bf16[1,8,512,512]{3,2,1,0:T(8,128)(2,1)} %act_hbm.1, s32[2,256]{1,0:T(2,128)} %bitcast.13, s32[32]{0:T(128)} %user_owner_hbm.1, s32[32]{0:T(128)} %item_owner_hbm.1, f32[32,512]{1,0:T(8,128)} %bitcast.9, f32[32,512]{1,0:T(8,128)} %bitcast.10, ...), custom_call_target="tpu_custom_call" | custom-call | tf_op jit(solution)/shard_map/sweep/pallas_call | solution.py:591
  111.3 1.6 %settle.1 = (f32[32,512]{1,0:T(8,128)}, f32[32,512]{1,0:T(8,128)}, f32[32,512]{1,0:T(8,128)}, f32[32,512]{1,0:T(8,128)}) custom-call(f32[32,512]{1,0:T(8,128)} %get-tuple-element.12.refs_0_, f32[32,512]{1,0:T(8,128)} %get-tuple-element.13.refs_1_, f32[32,512]{1,0:T(8,128)} %get-tuple-element.14.refs_2_, f32[32,512]{1,0:T(8,128)} %get-tuple-element.15.refs_3_), custom_call_target="tpu_custom_call" | custom-call | tf_op jit(solution)/shard_map/settle/pallas_call | solution.py:647

commit v3 on v2

--- a/solution.py
+++ b/solution.py
@@ -463,14 +463,14 @@
         gram = gram_line(p, gram)
         firsts = [spread(0, twins[0])]
         gram = gram_plane(p, gram)
+        twins.append(pass_on(1))
         penalty = inverse_start(p, gram)
-        inverse_steps(0, 2)
-        twins.append(pass_on(1))
+        inverse_steps(0, 1)
         seconds = [spread_on(0, firsts[0])]
-        inverse_steps(2, 3)
         firsts.append(spread(1, twins[1]))
+        inverse_steps(1, 3)
+        seconds.append(spread_on(1, firsts[1]))
         inverse_steps(3, 4)
-        seconds.append(spread_on(1, firsts[1]))
         inverse_steps(4, STEPS)
         return jnp.concatenate([finish(h, seconds[h]) for h in range(2)], axis=0), penalty
 

time: 113 us -> 113 us (level)
  no operation moved by 1% of the time
where the time goes in v3:
time: 113 us; the launch traced here: 112 us
  Pallas kernels  112 us (99%)
    pallas_call x1, Pallas kernels, local(): pl.pallas_call(sweep_kernel, out_shape=(slab,) * 4, in_specs=[hbm] * 9, o...  110 us

profile of v3, /device:TPU:1, one launch (start us, length us, event | category | flops | bytes accessed | tf_op | source)
XLA Modules:
  0.0 112.5 jit_solution(12419309203876991840)
XLA Ops:
  0.6 110.2 %sweep.1 = (f32[32,512]{1,0:T(8,128)}, f32[32,512]{1,0:T(8,128)}, f32[32,512]{1,0:T(8,128)}, f32[32,512]{1,0:T(8,128)}) custom-call(bf16[1,8,512,512]{3,2,1,0:T(8,128)(2,1)} %act_hbm.1, s32[2,256]{1,0:T(2,128)} %bitcast.13, s32[32]{0:T(128)} %user_owner_hbm.1, s32[32]{0:T(128)} %item_owner_hbm.1, f32[32,512]{1,0:T(8,128)} %bitcast.9, f32[32,512]{1,0:T(8,128)} %bitcast.10, ...), custom_call_target="tpu_custom_call" | custom-call | tf_op jit(solution)/shard_map/sweep/pallas_call | solution.py:591
  110.8 1.6 %settle.1 = (f32[32,512]{1,0:T(8,128)}, f32[32,512]{1,0:T(8,128)}, f32[32,512]{1,0:T(8,128)}, f32[32,512]{1,0:T(8,128)}) custom-call(f32[32,512]{1,0:T(8,128)} %get-tuple-element.12.refs_0_, f32[32,512]{1,0:T(8,128)} %get-tuple-element.13.refs_1_, f32[32,512]{1,0:T(8,128)} %get-tuple-element.14.refs_2_, f32[32,512]{1,0:T(8,128)} %get-tuple-element.15.refs_3_), custom_call_target="tpu_custom_call" | custom-call | tf_op jit(solution)/shard_map/settle/pallas_call | solution.py:647

commit v4 on v3

--- a/solution.py
+++ b/solution.py
@@ -176,8 +176,7 @@
 
     def take_rows():
         rows_group.take()
-        for a in range(4):
-            unpack(a)
+        unpack(0)
 
     def gather(p, halves, after_start, after_middle, after_plane):
         buf = gath.at[p]
@@ -532,7 +531,10 @@
     ).astype(F32)
     take_rows()
     gram_local(0, held[0])
-    gram = gram_twin(0, gram_y(0, gram_x(0)))
+    gram = gram_x(0)
+    for a in (1, 2, 3):
+        unpack(a)
+    gram = gram_twin(0, gram_y(0, gram))
     fetched.take()
     loads[8].wait()
     turned = jnp.concatenate(

time: 113 us -> 113 us (level)
  no operation moved by 1% of the time
where the time goes in v4:
time: 113 us; the launch traced here: 112 us
  Pallas kernels  112 us (99%)
    pallas_call x1, Pallas kernels, local(): pl.pallas_call(sweep_kernel, out_shape=(slab,) * 4, in_specs=[hbm] * 9, o...  110 us

profile of v4, /device:TPU:1, one launch (start us, length us, event | category | flops | bytes accessed | tf_op | source)
XLA Modules:
  0.0 112.5 jit_solution(7825420725323186850)
XLA Ops:
  0.6 110.2 %sweep.1 = (f32[32,512]{1,0:T(8,128)}, f32[32,512]{1,0:T(8,128)}, f32[32,512]{1,0:T(8,128)}, f32[32,512]{1,0:T(8,128)}) custom-call(bf16[1,8,512,512]{3,2,1,0:T(8,128)(2,1)} %act_hbm.1, s32[2,256]{1,0:T(2,128)} %bitcast.13, s32[32]{0:T(128)} %user_owner_hbm.1, s32[32]{0:T(128)} %item_owner_hbm.1, f32[32,512]{1,0:T(8,128)} %bitcast.9, f32[32,512]{1,0:T(8,128)} %bitcast.10, ...), custom_call_target="tpu_custom_call" | custom-call | tf_op jit(solution)/shard_map/sweep/pallas_call | solution.py:593
  110.8 1.6 %settle.1 = (f32[32,512]{1,0:T(8,128)}, f32[32,512]{1,0:T(8,128)}, f32[32,512]{1,0:T(8,128)}, f32[32,512]{1,0:T(8,128)}) custom-call(f32[32,512]{1,0:T(8,128)} %get-tuple-element.12.refs_0_, f32[32,512]{1,0:T(8,128)} %get-tuple-element.13.refs_1_, f32[32,512]{1,0:T(8,128)} %get-tuple-element.14.refs_2_, f32[32,512]{1,0:T(8,128)} %get-tuple-element.15.refs_3_), custom_call_target="tpu_custom_call" | custom-call | tf_op jit(solution)/shard_map/settle/pallas_call | solution.py:649
